TPU v7x, 256 devices: a whole 4x4x8 slice. The times are simulated.
256 devices in a mesh: island: 16 (over x, z_lo), expert: 4 (over y), fsdp: 4 (over z_hi, core).
Axes of the slice: x: 4, y: 4, z: 8 (z_hi: 2, z_lo: 4; z = z_hi * 4 + z_lo), core: 2. Of those that a mesh axis runs over, the one named last changes fastest.
Arguments:
- deltas: bfloat16 [16, 4, 4096, 1536], P('island', 'expert', 'fsdp'), may hold values from -6 to 6
- order: int32 [4], replicated, may hold values from 0 to 15
- staleness: int32 [16], replicated, may hold values from 0 to 15
- period: int32 [1], replicated, may hold values from 2 to 4
- counter: int32 [1], replicated, may hold values from 0 to 11
- theta: float32 [4, 4096, 1536], P('expert', ('fsdp', 'island')), may hold values from -6 to 6
- momentum: float32 [4, 4096, 1536], P('expert', ('fsdp', 'island')), may hold values from -4 to 4
- accum: float32 [4, 4096, 1536], P('expert', ('fsdp', 'island')), may hold values from -4 to 4
Outputs:
- fresh: bfloat16 [16, 4, 4096, 1536], P('island', 'expert', 'fsdp')
- theta_out: float32 [4, 4096, 1536], P('expert', ('fsdp', 'island'))
- momentum_out: float32 [4, 4096, 1536], P('expert', ('fsdp', 'island'))
- accum_out: float32 [4, 4096, 1536], P('expert', ('fsdp', 'island'))
All inputs are finite; a program needn't handle non-finite values.
Results may differ from a plain program's by a relative error of at most 0.001.
Values may be sent and summed in bfloat16 or wider, within the bound.
A program may use at most 128 MiB of HBM per device.

v0:
```python
import jax
import jax.numpy as jnp
from jax import lax
from jax.sharding import PartitionSpec as P


def spread(shard, axis, root):
    mine = lax.axis_index(axis) == root
    return lax.psum(jnp.where(mine, shard, jnp.zeros_like(shard)), axis)


def local(deltas, order, staleness, period, counter, theta, momentum, accum):
    rate = 0.7
    beta = 0.9
    islands = lax.axis_size("island")
    myself = lax.axis_index("island")
    mine = deltas[0]
    exp_loc, rows_all, width = mine.shape
    rows = rows_all // islands
    period_f = period[0].astype(jnp.float32)
    fresh = jnp.zeros(mine.shape, jnp.bfloat16)
    for k in range(order.shape[0]):
        source = order[k]
        whole = spread(mine, "island", source)
        piece = lax.dynamic_slice_in_dim(whole, myself * rows, rows, 1)
        weight = lax.rsqrt(1.0 + staleness[source].astype(jnp.float32) + k)
        grad = weight * piece.astype(jnp.float32)
        boundary = (counter[0] + k + 1) % period[0] == 0
        correction = 1.0 - jnp.power(jnp.float32(beta), (counter[0] + k + 1).astype(jnp.float32))
        momentum = jnp.where(boundary, beta * momentum + accum / period_f, momentum)
        accum = jnp.where(boundary, grad, accum + grad)
        theta = theta - rate * (
            grad + jnp.where(boundary, beta * momentum / correction, jnp.float32(0.0))
        )
        rounded = theta.astype(jnp.bfloat16)
        gathered = lax.all_gather(rounded, "island", axis=1, tiled=True)
        fresh = jnp.where(myself == source, gathered, fresh)
    return (fresh[None], theta, momentum, accum)


def solution(mesh):
    placed = (
        P("island", "expert", "fsdp", None),
        P(),
        P(),
        P(),
        P(),
        P("expert", ("fsdp", "island"), None),
        P("expert", ("fsdp", "island"), None),
        P("expert", ("fsdp", "island"), None),
    )
    return jax.shard_map(
        local,
        mesh=mesh,
        in_specs=placed,
        out_specs=(
            P("island", "expert", "fsdp", None),
            P("expert", ("fsdp", "island"), None),
            P("expert", ("fsdp", "island"), None),
            P("expert", ("fsdp", "island"), None),
        ),
        check_vma=False,
    )
```

profile of v0, /device:TPU:24, one launch (start us, length us, event | category | flops | bytes accessed | tf_op | source)
XLA Modules:
  0.0 954.0 jit_solution(10924398924033915100)
XLA Ops:
  7.2 0.0 all-reduce.3.cloned.1.call-start
  7.2 1.5 fusion.5
  11.3 6.2 select_bitcast_fusion.1
  17.4 0.0 copy-start.3
  17.4 0.0 copy-start
  17.4 0.0 copy-start.1
  17.4 0.0 copy-start.2
  17.4 0.0 all-reduce.3.cloned.1.call-update
  17.5 0.0 all-gather.5.cloned.1.call-start
  26.6 0.0 copy-done.3
  26.7 0.7 fusion.4
  30.4 537.1 %all-reduce.3.cloned.1.call-done = (bf16[1,1024,1536]{2,1,0:T(8,128)(2,1)}, bf16[1,1024,1536]{2,1,0:T(8,128)(2,1)}, bf16[1,1024,1536]{2,1,0:T(8,128)(2,1)}, bf16[1,1024,1536]{2,1,0:T(8,128)(2,1)}) async-done(((bf16[1,1024,1536]{2,1,0:T(8,128)(2,1)}, bf16[1,1024,1536]{2,1,0:T(8,128)(2,1)}, bf16[1,1024,1536]{2,1,0:T(8,128)(2,1)}, bf16[1,1024,1536]{2,1,0:T(8,128)(2,1)}), (bf16[1,1024,1536]{2,1,0:T(8,128)(2,1)}, ...) | async-done | bytes 12582928 | tf_op jit(solution)/shard_map/psum | solution.py:9
  567.5 0.0 copy-done
  567.5 0.0 copy-done.1
  567.5 0.0 copy-done.2
  567.5 1.8 fusion.1
  569.3 2.4 add_select_fusion
  571.7 2.0 fusion.2
  573.7 2.2 fusion.3
  575.9 0.0 all-gather.5.cloned.1.call-update
  575.9 0.0 all-gather.7.cloned.1.call-start
  576.0 0.7 all-gather.7.cloned.1.call-update
  576.6 0.0 all-gather.9.cloned.1.call-start
  576.7 0.5 all-gather.9.cloned.1.call-update
  577.2 0.0 all-gather.11.cloned.1.call-start
  577.3 0.5 all-gather.11.cloned.1.call-update
  577.8 90.3 %all-gather.5.cloned.1.call-done = bf16[1,1024,1536]{2,1,0:T(8,128)(2,1)} async-done(((bf16[1,64,1536]{2,1,0:T(8,128)(2,1)}), bf16[1,1024,1536]{2,1,0:T(8,128)(2,1)}) %all-gather.5.cloned.1.call-update) | async-done | bytes 3145744 | tf_op jit(solution)/shard_map/all_gather | solution.py:36
  668.1 91.7 %all-gather.7.cloned.1.call-done = bf16[1,1024,1536]{2,1,0:T(8,128)(2,1)} async-done(((bf16[1,64,1536]{2,1,0:T(8,128)(2,1)}), bf16[1,1024,1536]{2,1,0:T(8,128)(2,1)}) %all-gather.7.cloned.1.call-update) | async-done | bytes 3145744 | tf_op jit(solution)/shard_map/all_gather | solution.py:36
  759.8 91.5 %all-gather.9.cloned.1.call-done = bf16[1,1024,1536]{2,1,0:T(8,128)(2,1)} async-done(((bf16[1,64,1536]{2,1,0:T(8,128)(2,1)}), bf16[1,1024,1536]{2,1,0:T(8,128)(2,1)}) %all-gather.9.cloned.1.call-update) | async-done | bytes 3145744 | tf_op jit(solution)/shard_map/all_gather | solution.py:36
  851.3 92.1 %all-gather.11.cloned.1.call-done = bf16[1,1024,1536]{2,1,0:T(8,128)(2,1)} async-done(((bf16[1,64,1536]{2,1,0:T(8,128)(2,1)}), bf16[1,1024,1536]{2,1,0:T(8,128)(2,1)}) %all-gather.11.cloned.1.call-update) | async-done | bytes 3145744 | tf_op jit(solution)/shard_map/all_gather | solution.py:36
  943.4 4.1 select_bitcast_fusion
Async XLA Ops:
  7.2 560.3 %all-reduce.3.cloned.1.call-start = ((), (), s32[]{:S(2)}) async-start(), calls=%async_computation.4 | async-start | bytes 25165824 | tf_op jit(solution)/shard_map/psum | solution.py:9
  17.4 9.2 copy-start.3
  17.4 550.1 %copy-start = (f32[1,64,1536]{2,1,0:T(8,128)S(1)}, f32[1,64,1536]{2,1,0:T(8,128)}, u32[]{:S(2)}) copy-start(f32[1,64,1536]{2,1,0:T(8,128)} %param.15) | copy-start | bytes 1179652
  17.4 550.1 %copy-start.1 = (f32[1,64,1536]{2,1,0:T(8,128)S(1)}, f32[1,64,1536]{2,1,0:T(8,128)}, u32[]{:S(2)}) copy-start(f32[1,64,1536]{2,1,0:T(8,128)} %param.14) | copy-start | bytes 1179652
  17.4 550.1 %copy-start.2 = (f32[1,64,1536]{2,1,0:T(8,128)S(1)}, f32[1,64,1536]{2,1,0:T(8,128)}, u32[]{:S(2)}) copy-start(f32[1,64,1536]{2,1,0:T(8,128)} %param.13) | copy-start | bytes 1179652
  17.5 650.6 %all-gather.5.cloned.1.call-start = ((), (), s32[]{:S(2)}) async-start(), calls=%async_computation | async-start | bytes 3342336 | tf_op jit(solution)/shard_map/all_gather | solution.py:36
  575.9 183.9 %all-gather.7.cloned.1.call-start = ((), (), s32[]{:S(2)}) async-start(), calls=%async_computation.1 | async-start | bytes 3342336 | tf_op jit(solution)/shard_map/all_gather | solution.py:36
  576.6 274.6 %all-gather.9.cloned.1.call-start = ((), (), s32[]{:S(2)}) async-start(), calls=%async_computation.2 | async-start | bytes 3342336 | tf_op jit(solution)/shard_map/all_gather | solution.py:36
  577.2 366.2 %all-gather.11.cloned.1.call-start = ((), (), s32[]{:S(2)}) async-start(), calls=%async_computation.3 | async-start | bytes 3342336 | tf_op jit(solution)/shard_map/all_gather | solution.py:36
Sparse Core Ops, SparseCore 0:
  17.6 549.8 all-reduce.2
  576.0 92.0 all-gather.4
  669.9 89.8 all-gather.6
  761.4 89.8 all-gather.8
  853.5 89.8 all-gather.10
where the time goes:
time: 954 us
  waiting for transfers between devices  904 us (95%)
  between operations  28.5 us (3%)
  other arithmetic  18.7 us (2%)
    psum x1, waiting for transfers between devices, spread(): return lax.psum(jnp.where(mine, shard, jnp.zeros_like(shard)), axis)  537 us
    all_gather x4, waiting for transfers between devices, local(): gathered = lax.all_gather(rounded, 'island', axis=1, tiled=True)  366 us
  transfers between devices with their start and end apart: 5, of which 5 were waited for; matrix products, arithmetic and copies ran while one was open for 0% of the time, Pallas kernels for 0%

commit v1 on v0

v1 whole, which is shorter than its diff:
```python
import jax
import jax.numpy as jnp
from jax import lax
from jax.sharding import PartitionSpec as P


def local(deltas, order, staleness, period, counter, theta, momentum, accum):
    rate = 0.7
    beta = 0.9
    islands = lax.axis_size("island")
    rows_all, width = deltas.shape[2:]
    rows = rows_all // islands
    mine = deltas.reshape(islands, rows, width)
    pieces = lax.all_to_all(mine, "island", 0, 0, tiled=True)
    period_f = period[0].astype(jnp.float32)
    outgoing = jnp.zeros((islands, rows, width), jnp.bfloat16)
    for k in range(order.shape[0]):
        source = order[k]
        piece = lax.dynamic_index_in_dim(pieces, source, 0, keepdims=True)
        weight = lax.rsqrt(1.0 + staleness[source].astype(jnp.float32) + k)
        grad = weight * piece.astype(jnp.float32)
        boundary = (counter[0] + k + 1) % period[0] == 0
        correction = 1.0 - jnp.power(jnp.float32(beta), (counter[0] + k + 1).astype(jnp.float32))
        momentum = jnp.where(boundary, beta * momentum + accum / period_f, momentum)
        accum = jnp.where(boundary, grad, accum + grad)
        theta = theta - rate * (
            grad + jnp.where(boundary, beta * momentum / correction, jnp.float32(0.0))
        )
        outgoing = lax.dynamic_update_slice_in_dim(outgoing, theta.astype(jnp.bfloat16), source, 0)
    fresh = lax.all_to_all(outgoing, "island", 0, 0, tiled=True)
    return (fresh.reshape(deltas.shape), theta, momentum, accum)


def solution(mesh):
    state = P("expert", ("fsdp", "island"), None)
    replicas = P("island", "expert", "fsdp", None)
    return jax.shard_map(
        local,
        mesh=mesh,
        in_specs=(replicas, P(), P(), P(), P(), state, state, state),
        out_specs=(replicas, state, state, state),
        check_vma=False,
    )
```

time: 954 us -> 165 us (0.17)
  waiting for transfers between devices: 904 us -> 60.9 us
  blocking collectives: 0 us -> 74.9 us
  other arithmetic: 18.7 us -> 2.83 us
  between operations: 28.5 us -> 12.9 us
    psum x1 -> x0, waiting for transfers between devices: 537 us -> none  [spread(): return lax.psum(jnp.where(mine, shard, jnp.zeros_like(shard)), axis)]
    all_gather x4 -> x0, waiting for transfers between devices: 366 us -> none  [local(): gathered = lax.all_gather(rounded, 'island', axis=1, tiled=True)]
    all_to_all x0 -> x1, blocking collectives: none -> 74.9 us  [local(): fresh = lax.all_to_all(outgoing, 'island', 0, 0, tiled=True)]
    all_to_all x0 -> x1, waiting for transfers between devices: none -> 60.9 us  [local(): pieces = lax.all_to_all(mine, 'island', 0, 0, tiled=True)]
  transfers between devices with their start and end apart: 5 -> 1, of which waited for: 5 -> 1; matrix products, arithmetic and copies ran while one was open for 0% -> 1% of each run, Pallas kernels for 0% -> 0%
where the time goes in v1:
time: 165 us; the launch traced here: 164 us
  blocking collectives  74.9 us (45%)
  waiting for transfers between devices  60.9 us (37%)
  between operations  12.9 us (8%)
  starting transfers between devices  8.61 us (5%)
  local copies, waits for them, and re-layouts  3.98 us (2%)
  other arithmetic  2.83 us (2%)
    all_to_all x1, blocking collectives, local(): fresh = lax.all_to_all(outgoing, 'island', 0, 0, tiled=True)  74.9 us
    all_to_all x1, waiting for transfers between devices, local(): pieces = lax.all_to_all(mine, 'island', 0, 0, tiled=True)  60.9 us
    all_to_all x1, starting transfers between devices, local(): pieces = lax.all_to_all(mine, 'island', 0, 0, tiled=True)  8.61 us
  transfers between devices with their start and end apart: 1, of which 1 were waited for; matrix products, arithmetic and copies ran while one was open for 1% of the time, Pallas kernels for 0%

profile of v1, /device:TPU:24, one launch (start us, length us, event | category | flops | bytes accessed | tf_op | source)
XLA Modules:
  0.0 164.1 jit_solution(414291973376736055)
XLA Ops:
  0.6 0.0 copy-start.4
  0.6 0.0 copy-start.3
  0.7 8.6 %all-to-all-start = ((bf16[16,64,1536]{2,1,0:T(8,128)(2,1)}), bf16[16,64,1536]{2,1,0:T(8,128)(2,1)S(1)}, u32[]{:S(2)}, u32[]{:S(2)}) async-start(bf16[16,64,1536]{2,1,0:T(8,128)(2,1)} %bitcast.19), calls=%async_computation | async-start | bytes 6291456 | tf_op jit(solution)/shard_map/all_to_all | solution.py:14
  9.3 0.0 copy-start
  10.7 0.0 copy-done.4
  10.7 0.6 fusion.1
  19.3 0.0 copy-done.3
  19.3 0.6 fusion
  22.7 60.9 %all-to-all-done = bf16[16,64,1536]{2,1,0:T(8,128)(2,1)S(1)} async-done(((bf16[16,64,1536]{2,1,0:T(8,128)(2,1)}), bf16[16,64,1536]{2,1,0:T(8,128)(2,1)S(1)}, u32[]{:S(2)}, u32[]{:S(2)}) %all-to-all-start) | async-done | bytes 3145760 | tf_op jit(solution)/shard_map/all_to_all | solution.py:14
  83.6 0.0 copy-start.1
  83.6 0.0 copy-start.2
  83.6 0.3 broadcast_in_dim.10
  83.9 0.0 copy-done
  83.9 0.7 copy-done.1
  84.6 0.1 copy-done.2
  84.7 0.2 convert_dynamic-update-slice_fusion.3
  84.9 0.3 convert_dynamic-update-slice_fusion.2
  85.2 1.0 add_select_fusion
  86.1 0.3 convert_dynamic-update-slice_fusion.1
  86.4 1.1 convert_dynamic-update-slice_fusion
  87.6 74.9 %all_to_all.10 = bf16[16,64,1536]{2,1,0:T(8,128)(2,1)S(1)} all-to-all(bf16[16,64,1536]{2,1,0:T(8,128)(2,1)S(1)} %get-tuple-element.6), channel_id=1, replica_groups=mesh['island'=16,'expert'=4,'fsdp'=4] {'island'}, dimensions={0} | all-to-all | bytes 6291456 | tf_op jit(solution)/shard_map/all_to_all | solution.py:30
  162.5 1.7 %copy.19 = bf16[1,1,1024,1536]{3,2,1,0:T(8,128)(2,1)} copy(bf16[1,1,1024,1536]{3,2,1,0:T(8,128)(2,1)S(1)} %bitcast.18) | data formatting | bytes 6291456
Async XLA Ops:
  0.6 10.1 %copy-start.4 = (s32[4]{0:T(128)S(1)}, s32[4]{0:T(128)}, u32[]{:S(2)}) copy-start(s32[4]{0:T(128)} %param.9) | copy-start | bytes 52
  0.6 18.7 %copy-start.3 = (s32[16]{0:T(128)S(1)}, s32[16]{0:T(128)}, u32[]{:S(2)}) copy-start(s32[16]{0:T(128)} %param.10) | copy-start | bytes 196
  0.7 83.0 %all-to-all-start = ((bf16[16,64,1536]{2,1,0:T(8,128)(2,1)}), bf16[16,64,1536]{2,1,0:T(8,128)(2,1)S(1)}, u32[]{:S(2)}, u32[]{:S(2)}) async-start(bf16[16,64,1536]{2,1,0:T(8,128)(2,1)} %bitcast.19), calls=%async_computation | async-start | bytes 6291456 | tf_op jit(solution)/shard_map/all_to_all | solution.py:14
  9.3 74.6 %copy-start = (f32[1,64,1536]{2,1,0:T(8,128)S(1)}, f32[1,64,1536]{2,1,0:T(8,128)}, u32[]{:S(2)}) copy-start(f32[1,64,1536]{2,1,0:T(8,128)} %param.15) | copy-start | bytes 1179652
  83.6 1.0 copy-start.1
  83.6 1.1 copy-start.2

commit v2 on v1

v2 whole, which is shorter than its diff:
```python
import functools

import jax
import jax.numpy as jnp
from jax import lax
from jax.experimental import pallas as pl
from jax.experimental.pallas import tpu as pltpu
from jax.sharding import PartitionSpec as P

RATE = 0.7
BETA = 0.9
LOG_BETA = -0.10536051565782628
ARRIVALS = 4
SIDE = 4
STEP = 16
HALVES = 1
LEAD = 1
MESH = pl.DeviceIdType.MESH


def column_tile(width):
    return 512 if width % 512 == 0 else 128


def kernel(slots, chunks, deltas, order, staleness, period, counter, theta, momentum, accum,
           fresh, theta_out, momentum_out, accum_out,
           landed, packed, pieces, rounded, answers, returned, outgoing, send, recv, near):
    me = lax.axis_index("island")
    x, z = me // SIDE, me % SIDE

    def along_x(d):
        return {"island": ((x + d) % SIDE) * SIDE + z}

    def along_z(d):
        return {"island": x * SIDE + (z + d) % SIDE}

    def remote(stage, j, d, src, dst, where):
        at = (stage * len(chunks) + j) * (SIDE - 1) + d - 1
        return pltpu.make_async_remote_copy(
            src_ref=src, dst_ref=dst, send_sem=send.at[at], recv_sem=recv.at[at],
            device_id=where, device_id_type=MESH)

    def block(j, column):
        row, col, wide = chunks[j]
        return (pl.ds(column * SIDE, SIDE), pl.ds(row, STEP), pl.ds(col, wide))

    def spread(j, d):
        return remote(0, j, d, deltas.at[block(j, (x + d) % SIDE)], landed[j].at[d], along_x(d))

    def spread_own(j):
        return pltpu.make_async_copy(deltas.at[block(j, x)], landed[j].at[0], near.at[j])

    def hand(j, d):
        return remote(1, j, d, packed[j].at[d], pieces[j].at[d], along_z(d))

    def answer(j, d):
        return remote(2, j, d, answers[j].at[d], returned[j].at[d], along_z(d))

    def deliver(j, d):
        return remote(3, j, d, outgoing[j].at[d], fresh.at[block(j, x)], along_x(d))

    def deliver_own(j):
        return pltpu.make_async_copy(outgoing[j].at[0], fresh.at[block(j, x)], near.at[len(chunks) + j])

    barrier = pltpu.get_barrier_semaphore()
    for d in range(1, SIDE):
        pl.semaphore_signal(barrier, inc=1, device_id=along_x(d), device_id_type=MESH)
        pl.semaphore_signal(barrier, inc=1, device_id=along_z(d), device_id_type=MESH)
    pl.semaphore_wait(barrier, 2 * (SIDE - 1))

    def start_spread(j):
        for d in range(1, SIDE):
            spread(j, d).start()
        spread_own(j).start()

    for j in range(min(LEAD, len(chunks))):
        start_spread(j)

    zero = jnp.int32(0)
    who = [order[k] for k in range(ARRIVALS)]
    col = [w // SIDE for w in who]
    plane = [w % SIDE for w in who]
    slot, first = [], []
    for k in range(ARRIVALS):
        again, rank = zero, zero
        same = zero
        for l in range(k):
            hit = (who[l] == who[k]).astype(jnp.int32)
            again = jnp.maximum(again, hit)
            same = jnp.where(hit == 1, slot[l], same)
            rank = rank + first[l] * (plane[l] == plane[k]).astype(jnp.int32)
        first.append(1 - again)
        slot.append(jnp.where(again == 1, same, rank))

    def held(at_plane, s):
        return [((plane[k] == at_plane) & (slot[k] == s)) for k in range(ARRIVALS)]

    mine = []
    for s in range(slots):
        value = zero
        for k, hit in enumerate(held(z, s)):
            value = jnp.where(hit, (x - col[k] + SIDE) % SIDE, value)
        mine.append(value)
    last = []
    for d in range(SIDE):
        row = []
        for s in range(slots):
            value = zero
            for k, hit in enumerate(held((z + d) % SIDE, s)):
                value = jnp.where(hit, jnp.int32(k), value)
            row.append(value)
        last.append(row)
    place = []
    for d in range(SIDE):
        value = jnp.int32(-1)
        for k in range(ARRIVALS):
            value = jnp.where((plane[k] == z) & (col[k] == (x + d) % SIDE), slot[k], value)
        place.append(value)
    origin = [(z - plane[k] + SIDE) % SIDE for k in range(ARRIVALS)]

    def pack(j):
        for d in range(1, SIDE):
            spread(j, d).wait_recv()
        spread_own(j).wait()
        for d in (2, 1, 3, 0):
            target = pieces[j] if d == 0 else packed[j]
            for s in range(slots):
                target[d, s] = landed[j][mine[s], (z + d) % SIDE]
            if d:
                hand(j, d).start()

    count = counter[0]
    every = period[0]

    def update(j):
        for d in range(1, SIDE):
            hand(j, d).wait_recv()
        row, begin, wide = chunks[j]
        tile = column_tile(wide)
        for start in range(0, wide, tile):
            here = (pl.ds(row, STEP), pl.ds(begin + start, tile))
            part = pl.ds(start, tile)
            th, mo, ac = theta[here], momentum[here], accum[here]
            one = jnp.ones((1, tile), jnp.float32)
            inverse = 1.0 / (one * every.astype(jnp.float32))
            for k in range(ARRIVALS):
                weight = lax.rsqrt(one * (1.0 + staleness[who[k]].astype(jnp.float32) + k))
                step = count + (k + 1)
                boundary = lax.rem(step, every) == 0
                factor = BETA / (1.0 - jnp.exp(one * (step.astype(jnp.float32) * LOG_BETA)))
                piece = pieces[j][origin[k], slot[k], :, part]
                grad = weight * piece.astype(jnp.float32)
                mo = jnp.where(boundary, BETA * mo + ac * inverse, mo)
                ac = jnp.where(boundary, grad, ac + grad)
                th = th - RATE * (grad + jnp.where(boundary, factor * mo, 0.0))
                rounded[j][k, :, part] = th.astype(jnp.bfloat16)
            theta_out[here], momentum_out[here], accum_out[here] = th, mo, ac
        for d in (2, 1, 3, 0):
            target = returned[j] if d == 0 else answers[j]
            for s in range(slots):
                target[d, s] = rounded[j][last[d][s]]
            if d:
                answer(j, d).start()

    def forward(j):
        for d in range(1, SIDE):
            answer(j, d).wait_recv()
        for d in (2, 1, 3, 0):
            keep = place[d] >= 0
            at = jnp.maximum(place[d], 0)
            for owner in range(SIDE):
                block = returned[j][(z - owner + SIDE) % SIDE, at]
                outgoing[j][d, owner] = jnp.where(keep, block, jnp.zeros_like(block))
            if d:
                deliver(j, d).start()
            else:
                deliver_own(j).start()

    total = len(chunks)
    for t in range(total + 2):
        if t + LEAD < total:
            start_spread(t + LEAD)
        if t < total:
            pack(t)
        if 0 <= t - 1 < total:
            update(t - 1)
        if 0 <= t - 2 < total:
            forward(t - 2)
    for j in range(total):
        for d in range(1, SIDE):
            deliver(j, d).wait_recv()
            for stage in (spread, hand, answer, deliver):
                stage(j, d).wait_send()
        deliver_own(j).wait()


def run(slots, tag, deltas, order, staleness, period, counter, theta, momentum, accum):
    islands, rows, width = deltas.shape
    wide = width // HALVES
    chunks = [(r, c * wide, wide) for r in range(0, rows, STEP) for c in range(HALVES)]
    n = len(chunks)
    copies = 4 * n * (SIDE - 1)
    smem = pl.BlockSpec(memory_space=pltpu.SMEM)
    vmem = pl.BlockSpec(memory_space=pltpu.VMEM)
    hbm = pl.BlockSpec(memory_space=pl.ANY)
    half = lambda *lead: [pltpu.VMEM((*lead, STEP, wide), jnp.bfloat16) for _ in range(n)]
    state = jax.ShapeDtypeStruct(theta.shape, jnp.float32)
    return pl.pallas_call(
        functools.partial(kernel, slots, chunks),
        out_shape=(jax.ShapeDtypeStruct(deltas.shape, jnp.bfloat16), state, state, state),
        in_specs=[hbm, smem, smem, smem, smem, vmem, vmem, vmem],
        out_specs=(hbm, vmem, vmem, vmem),
        scratch_shapes=[
            half(SIDE, SIDE),
            half(SIDE, slots),
            half(SIDE, slots),
            half(ARRIVALS),
            half(SIDE, slots),
            half(SIDE, slots),
            half(SIDE, SIDE),
            pltpu.SemaphoreType.DMA((copies,)),
            pltpu.SemaphoreType.DMA((copies,)),
            pltpu.SemaphoreType.DMA((2 * n,)),
        ],
        compiler_params=pltpu.CompilerParams(
            collective_id=tag, has_side_effects=True, vmem_limit_bytes=48 * 1024 * 1024
        ),
    )(deltas, order, staleness, period, counter, theta, momentum, accum)


def local(deltas, order, staleness, period, counter, theta, momentum, accum):
    islands = lax.axis_size("island")
    rows_all, width = deltas.shape[2:]
    blocks = deltas.reshape(islands, rows_all // islands, width)
    replica = jnp.arange(islands)
    arrives = (order[:, None] == replica[None, :]).any(0)
    crowd = arrives.reshape(SIDE, SIDE).sum(0).max()
    args = (blocks, order, staleness, period, counter, theta[0], momentum[0], accum[0])
    fresh, theta, momentum, accum = lax.cond(
        crowd <= 2, functools.partial(run, 2, 0), functools.partial(run, ARRIVALS, 1), *args
    )
    return (fresh.reshape(deltas.shape), theta[None], momentum[None], accum[None])


def solution(mesh):
    state = P("expert", ("fsdp", "island"), None)
    replicas = P("island", "expert", "fsdp", None)
    return jax.shard_map(
        local,
        mesh=mesh,
        in_specs=(replicas, P(), P(), P(), P(), state, state, state),
        out_specs=(replicas, state, state, state),
        check_vma=False,
    )
```

time: 165 us -> 108 us (0.65)
  Pallas kernels: 0 us -> 99.5 us
  blocking collectives: 74.9 us -> 0 us
  waiting for transfers between devices: 60.9 us -> 0 us
  between operations: 12.9 us -> 1.3 us
  starting transfers between devices: 8.61 us -> 0 us
    pallas_call x0 -> x1, Pallas kernels: none -> 99.5 us  [run(): pl.pallas_call(functools.partial(kernel, slots, chunks), out_shape=(jax.S...]
    all_to_all x1 -> x0, blocking collectives: 74.9 us -> none  [local(): fresh = lax.all_to_all(outgoing, 'island', 0, 0, tiled=True)]
    all_to_all x1 -> x0, waiting for transfers between devices: 60.9 us -> none  [local(): pieces = lax.all_to_all(mine, 'island', 0, 0, tiled=True)]
    all_to_all x1 -> x0, starting transfers between devices: 8.61 us -> none  [local(): pieces = lax.all_to_all(mine, 'island', 0, 0, tiled=True)]
    dynamic_update_slice x4 -> x0, other arithmetic: 1.87 us -> none  [local(): lax.dynamic_update_slice_in_dim(outgoing, theta.astype(jnp.bfloat16), sou...]
    unnamed x11 -> x4, local copies, waits for them, and re-layouts: 2.48 us -> 3.9 us
  transfers between devices with their start and end apart: 1 -> 0, of which waited for: 1 -> 0; matrix products, arithmetic and copies ran while one was open for 1% -> 0% of each run, Pallas kernels for 0% -> 0%
where the time goes in v2:
time: 108 us; the launch traced here: 106 us
  Pallas kernels  99.5 us (92%)
  local copies, waits for them, and re-layouts  3.99 us (4%)
  other arithmetic  1.41 us (1%)
  between operations  1.3 us (1%)
    pallas_call x1, Pallas kernels, run(): pl.pallas_call(functools.partial(kernel, slots, chunks), out_shape=(jax.S...  99.5 us
    unnamed x4, local copies, waits for them, and re-layouts  3.9 us

profile of v2, /device:TPU:24, one launch (start us, length us, event | category | flops | bytes accessed | tf_op | source)
XLA Modules:
  0.0 106.2 jit_solution(6197986136743607510)
XLA Ops:
  0.6 0.7 fusion
  1.4 0.1 reshape.24
  1.5 0.6 reduce_max.9
  2.8 99.5 %conditional.1 = ((bf16[16,64,1536]{2,1,0:T(8,128)(2,1)S(1)}, f32[64,1536]{1,0:T(8,128)S(1)}, f32[64,1536]{1,0:T(8,128)S(1)}, f32[64,1536]{1,0:T(8,128)S(1)})) conditional(s32[]{:T(128)} %convert_element_type.11, (bf16[16,64,1536]{2,1,0:T(8,128)(2,1)}, s32[4]{0:T(128)}, s32[16]{0:T(128)}, s32[1]{0:T(128)}, s32[1]{0:T(128)}, ...), branch_computations={%region_3.0_spmd, %region_4.0_spmd} | conditional | bytes 8 | solution.py:239
  2.8 99.5 %branch_1_fun.1 = (bf16[16,64,1536]{2,1,0:T(8,128)(2,1)S(1)}, f32[64,1536]{1,0:T(8,128)S(1)}, f32[64,1536]{1,0:T(8,128)S(1)}, f32[64,1536]{1,0:T(8,128)S(1)}) custom-call(bf16[16,64,1536]{2,1,0:T(8,128)(2,1)} %get-tuple-element.56.deltas, s32[4]{0:T(128)} %get-tuple-element.57.order, s32[16]{0:T(128)} %get-tuple-element.58.staleness, ...), custom_call_target="tpu_custom_call" | custom-call | tf_op jit(solution)/shard_map/cond/branch_1_fun/pallas_call | solution.py:208
  102.3 1.7 %copy.24 = bf16[1,1,1024,1536]{3,2,1,0:T(8,128)(2,1)} copy(bf16[1,1,1024,1536]{3,2,1,0:T(8,128)(2,1)S(1)} %bitcast.10) | data formatting | bytes 6291456
  103.9 0.7 copy.25
  104.7 0.7 copy.26
  105.4 0.7 copy.27
  (2 shorter events, 0.0 us)

commit v3 on v2

--- a/solution.py
+++ b/solution.py
@@ -13,8 +13,9 @@
 ARRIVALS = 4
 SIDE = 4
 STEP = 16
-HALVES = 1
-LEAD = 1
+HALVES = 2
+LEAD = 3
+PLANS = ((2, 1, 1, 2), (1, 2, 2, 1), (2, 2, 2, 2), (4, 4, 4, 4))
 MESH = pl.DeviceIdType.MESH
 
 
@@ -22,11 +23,20 @@
     return 512 if width % 512 == 0 else 128
 
 
-def kernel(slots, chunks, deltas, order, staleness, period, counter, theta, momentum, accum,
+def kernel(room, chunks, deltas, order, staleness, period, counter, theta, momentum, accum,
            fresh, theta_out, momentum_out, accum_out,
            landed, packed, pieces, rounded, answers, returned, outgoing, send, recv, near):
     me = lax.axis_index("island")
     x, z = me // SIDE, me % SIDE
+    slots, least = max(room), min(room)
+    groups = [(0, least)] + [(s, 1) for s in range(least, slots)]
+
+    def where_room(s, plane, go):
+        if s < least:
+            go()
+        else:
+            has = functools.reduce(jnp.logical_or, [plane == p for p in range(SIDE) if room[p] > s])
+            pl.when(has)(go)
 
     def along_x(d):
         return {"island": ((x + d) % SIDE) * SIDE + z}
@@ -35,9 +45,9 @@
         return {"island": x * SIDE + (z + d) % SIDE}
 
     def remote(stage, j, d, src, dst, where):
-        at = (stage * len(chunks) + j) * (SIDE - 1) + d - 1
+        at = stage * (SIDE - 1) + d - 1
         return pltpu.make_async_remote_copy(
-            src_ref=src, dst_ref=dst, send_sem=send.at[at], recv_sem=recv.at[at],
+            src_ref=src, dst_ref=dst, send_sem=send.at[j, at], recv_sem=recv.at[j, at],
             device_id=where, device_id_type=MESH)
 
     def block(j, column):
@@ -50,14 +60,20 @@
     def spread_own(j):
         return pltpu.make_async_copy(deltas.at[block(j, x)], landed[j].at[0], near.at[j])
 
-    def hand(j, d):
-        return remote(1, j, d, packed[j].at[d], pieces[j].at[d], along_z(d))
-
-    def answer(j, d):
-        return remote(2, j, d, answers[j].at[d], returned[j].at[d], along_z(d))
+    def hand(j, d, g):
+        part = pl.ds(*groups[g])
+        return remote(2 + g, j, d, packed[j].at[d, part], pieces[j].at[d, part], along_z(d))
+
+    def answer(j, d, g):
+        part = pl.ds(*groups[g])
+        return remote(2 + len(groups) + g, j, d, answers[j].at[d, part], returned[j].at[d, part], along_z(d))
+
+    def over_groups(plane, act):
+        for g, (s, _) in enumerate(groups):
+            where_room(s, plane, functools.partial(act, g))
 
     def deliver(j, d):
-        return remote(3, j, d, outgoing[j].at[d], fresh.at[block(j, x)], along_x(d))
+        return remote(1, j, d, outgoing[j].at[d], fresh.at[block(j, x)], along_x(d))
 
     def deliver_own(j):
         return pltpu.make_async_copy(outgoing[j].at[0], fresh.at[block(j, x)], near.at[len(chunks) + j])
@@ -127,14 +143,14 @@
             for s in range(slots):
                 target[d, s] = landed[j][mine[s], (z + d) % SIDE]
             if d:
-                hand(j, d).start()
+                over_groups(z, lambda g, d=d: hand(j, d, g).start())
 
     count = counter[0]
     every = period[0]
 
     def update(j):
         for d in range(1, SIDE):
-            hand(j, d).wait_recv()
+            over_groups((z + SIDE - d) % SIDE, lambda g, d=d: hand(j, d, g).wait_recv())
         row, begin, wide = chunks[j]
         tile = column_tile(wide)
         for start in range(0, wide, tile):
@@ -160,11 +176,11 @@
             for s in range(slots):
                 target[d, s] = rounded[j][last[d][s]]
             if d:
-                answer(j, d).start()
+                over_groups((z + d) % SIDE, lambda g, d=d: answer(j, d, g).start())
 
     def forward(j):
         for d in range(1, SIDE):
-            answer(j, d).wait_recv()
+            over_groups(z, lambda g, d=d: answer(j, d, g).wait_recv())
         for d in (2, 1, 3, 0):
             keep = place[d] >= 0
             at = jnp.maximum(place[d], 0)
@@ -189,24 +205,28 @@
     for j in range(total):
         for d in range(1, SIDE):
             deliver(j, d).wait_recv()
-            for stage in (spread, hand, answer, deliver):
-                stage(j, d).wait_send()
+            spread(j, d).wait_send()
+            deliver(j, d).wait_send()
+            over_groups(z, lambda g, d=d: hand(j, d, g).wait_send())
+            over_groups((z + d) % SIDE, lambda g, d=d: answer(j, d, g).wait_send())
         deliver_own(j).wait()
 
 
-def run(slots, tag, deltas, order, staleness, period, counter, theta, momentum, accum):
+def run(room, tag, deltas, order, staleness, period, counter, theta, momentum, accum):
     islands, rows, width = deltas.shape
     wide = width // HALVES
     chunks = [(r, c * wide, wide) for r in range(0, rows, STEP) for c in range(HALVES)]
     n = len(chunks)
-    copies = 4 * n * (SIDE - 1)
+    slots = max(room)
+    stages = 2 + 2 * (1 + slots - min(room))
+    copies = (n, stages * (SIDE - 1))
     smem = pl.BlockSpec(memory_space=pltpu.SMEM)
     vmem = pl.BlockSpec(memory_space=pltpu.VMEM)
     hbm = pl.BlockSpec(memory_space=pl.ANY)
     half = lambda *lead: [pltpu.VMEM((*lead, STEP, wide), jnp.bfloat16) for _ in range(n)]
     state = jax.ShapeDtypeStruct(theta.shape, jnp.float32)
     return pl.pallas_call(
-        functools.partial(kernel, slots, chunks),
+        functools.partial(kernel, room, chunks),
         out_shape=(jax.ShapeDtypeStruct(deltas.shape, jnp.bfloat16), state, state, state),
         in_specs=[hbm, smem, smem, smem, smem, vmem, vmem, vmem],
         out_specs=(hbm, vmem, vmem, vmem),
@@ -218,8 +238,8 @@
             half(SIDE, slots),
             half(SIDE, slots),
             half(SIDE, SIDE),
-            pltpu.SemaphoreType.DMA((copies,)),
-            pltpu.SemaphoreType.DMA((copies,)),
+            pltpu.SemaphoreType.DMA(copies),
+            pltpu.SemaphoreType.DMA(copies),
             pltpu.SemaphoreType.DMA((2 * n,)),
         ],
         compiler_params=pltpu.CompilerParams(
@@ -232,13 +252,12 @@
     islands = lax.axis_size("island")
     rows_all, width = deltas.shape[2:]
     blocks = deltas.reshape(islands, rows_all // islands, width)
-    replica = jnp.arange(islands)
-    arrives = (order[:, None] == replica[None, :]).any(0)
-    crowd = arrives.reshape(SIDE, SIDE).sum(0).max()
+    arrives = (order[:, None] == jnp.arange(islands)[None, :]).any(0)
+    crowd = arrives.reshape(SIDE, SIDE).sum(0)
     args = (blocks, order, staleness, period, counter, theta[0], momentum[0], accum[0])
-    fresh, theta, momentum, accum = lax.cond(
-        crowd <= 2, functools.partial(run, 2, 0), functools.partial(run, ARRIVALS, 1), *args
-    )
+    branches = [functools.partial(run, room, tag) for tag, room in enumerate(PLANS)]
+    fits = (crowd[None, :] <= jnp.array(PLANS)).all(1)
+    fresh, theta, momentum, accum = lax.switch(jnp.argmax(fits).astype(jnp.int32), branches, *args)
     return (fresh.reshape(deltas.shape), theta[None], momentum[None], accum[None])
 
 

time: 108 us -> 166 us (1.54)
  Pallas kernels: 99.5 us -> 157 us
    pallas_call x1, Pallas kernels: 99.5 us -> 157 us  [run(): pl.pallas_call(functools.partial(kernel, room, chunks), out_shape=(jax.Sh...]
where the time goes in v3:
time: 166 us; the launch traced here: 165 us
  Pallas kernels  157 us (95%)
  local copies, waits for them, and re-layouts  3.99 us (2%)
  other arithmetic  2.23 us (1%)
    pallas_call x1, Pallas kernels, run(): pl.pallas_call(functools.partial(kernel, room, chunks), out_shape=(jax.Sh...  157 us
    unnamed x4, local copies, waits for them, and re-layouts  3.9 us

profile of v3, /device:TPU:24, one launch (start us, length us, event | category | flops | bytes accessed | tf_op | source)
XLA Modules:
  0.0 165.2 jit_solution(15919925697453598480)
XLA Ops:
  0.6 0.7 fusion
  1.4 0.1 reshape.31
  1.5 0.8 compare_reduce_fusion
  2.3 0.7 iota_reduce_fusion
  3.6 157.7 %conditional.1 = ((bf16[16,64,1536]{2,1,0:T(8,128)(2,1)S(1)}, f32[64,1536]{1,0:T(8,128)S(1)}, f32[64,1536]{1,0:T(8,128)S(1)}, f32[64,1536]{1,0:T(8,128)S(1)})) conditional(s32[]{:T(128)} %clamp.3, (bf16[16,64,1536]{2,1,0:T(8,128)(2,1)}, s32[4]{0:T(128)}, s32[16]{0:T(128)}, s32[1]{0:T(128)}, s32[1]{0:T(128)}, ...), branch_computations={%region_4.5_spmd, %region_5.6_spmd, %region_6.7_spmd, %region_7.8_... | conditional | bytes 8 | solution.py:260
  3.8 157.3 %branch_3_fun.1 = (bf16[16,64,1536]{2,1,0:T(8,128)(2,1)S(1)}, f32[64,1536]{1,0:T(8,128)S(1)}, f32[64,1536]{1,0:T(8,128)S(1)}, f32[64,1536]{1,0:T(8,128)S(1)}) custom-call(bf16[16,64,1536]{2,1,0:T(8,128)(2,1)} %get-tuple-element.120.deltas, s32[4]{0:T(128)} %get-tuple-element.121.order, s32[16]{0:T(128)} %get-tuple-element.122.staleness, ...), custom_call_target="tpu_custom_call" | custom-call | tf_op jit(solution)/shard_map/cond/branch_3_fun/pallas_call | solution.py:228
  161.3 1.7 %copy.33 = bf16[1,1,1024,1536]{3,2,1,0:T(8,128)(2,1)} copy(bf16[1,1,1024,1536]{3,2,1,0:T(8,128)(2,1)S(1)} %bitcast.24) | data formatting | bytes 6291456
  163.0 0.7 copy.34
  163.7 0.7 copy.35
  164.5 0.7 copy.36
  (2 shorter events, 0.0 us)

commit v4 on v3

--- a/solution.py
+++ b/solution.py
@@ -16,6 +16,7 @@
 HALVES = 2
 LEAD = 3
 PLANS = ((2, 1, 1, 2), (1, 2, 2, 1), (2, 2, 2, 2), (4, 4, 4, 4))
+SETTLE = 2
 MESH = pl.DeviceIdType.MESH
 
 
@@ -25,7 +26,7 @@
 
 def kernel(room, chunks, deltas, order, staleness, period, counter, theta, momentum, accum,
            fresh, theta_out, momentum_out, accum_out,
-           landed, packed, pieces, rounded, answers, returned, outgoing, send, recv, near):
+           state, landed, packed, pieces, rounded, answers, returned, outgoing, send, recv, near, moved):
     me = lax.axis_index("island")
     x, z = me // SIDE, me % SIDE
     slots, least = max(room), min(room)
@@ -77,6 +78,18 @@
 
     def deliver_own(j):
         return pltpu.make_async_copy(outgoing[j].at[0], fresh.at[block(j, x)], near.at[len(chunks) + j])
+
+    theta_now, momentum_now, accum_now = state
+    loads = [pltpu.make_async_copy(src, dst, moved.at[len(chunks), i])
+             for i, (src, dst) in enumerate(zip((theta, momentum, accum), state))]
+    for load in loads:
+        load.start()
+
+    def store(j):
+        row, col, wide = chunks[j]
+        here = (pl.ds(row, STEP), pl.ds(col, wide))
+        return [pltpu.make_async_copy(src.at[here], dst.at[here], moved.at[j, i])
+                for i, (src, dst) in enumerate(zip(state, (theta_out, momentum_out, accum_out)))]
 
     barrier = pltpu.get_barrier_semaphore()
     for d in range(1, SIDE):
@@ -151,12 +164,15 @@
     def update(j):
         for d in range(1, SIDE):
             over_groups((z + SIDE - d) % SIDE, lambda g, d=d: hand(j, d, g).wait_recv())
+        if j == 0:
+            for load in loads:
+                load.wait()
         row, begin, wide = chunks[j]
         tile = column_tile(wide)
         for start in range(0, wide, tile):
             here = (pl.ds(row, STEP), pl.ds(begin + start, tile))
             part = pl.ds(start, tile)
-            th, mo, ac = theta[here], momentum[here], accum[here]
+            th, mo, ac = theta_now[here], momentum_now[here], accum_now[here]
             one = jnp.ones((1, tile), jnp.float32)
             inverse = 1.0 / (one * every.astype(jnp.float32))
             for k in range(ARRIVALS):
@@ -170,7 +186,7 @@
                 ac = jnp.where(boundary, grad, ac + grad)
                 th = th - RATE * (grad + jnp.where(boundary, factor * mo, 0.0))
                 rounded[j][k, :, part] = th.astype(jnp.bfloat16)
-            theta_out[here], momentum_out[here], accum_out[here] = th, mo, ac
+            theta_now[here], momentum_now[here], accum_now[here] = th, mo, ac
         for d in (2, 1, 3, 0):
             target = returned[j] if d == 0 else answers[j]
             for s in range(slots):
@@ -181,6 +197,8 @@
     def forward(j):
         for d in range(1, SIDE):
             over_groups(z, lambda g, d=d: answer(j, d, g).wait_recv())
+        for copy in store(j):
+            copy.start()
         for d in (2, 1, 3, 0):
             keep = place[d] >= 0
             at = jnp.maximum(place[d], 0)
@@ -210,6 +228,8 @@
             over_groups(z, lambda g, d=d: hand(j, d, g).wait_send())
             over_groups((z + d) % SIDE, lambda g, d=d: answer(j, d, g).wait_send())
         deliver_own(j).wait()
+        for copy in store(j):
+            copy.wait()
 
 
 def run(room, tag, deltas, order, staleness, period, counter, theta, momentum, accum):
@@ -221,16 +241,16 @@
     stages = 2 + 2 * (1 + slots - min(room))
     copies = (n, stages * (SIDE - 1))
     smem = pl.BlockSpec(memory_space=pltpu.SMEM)
-    vmem = pl.BlockSpec(memory_space=pltpu.VMEM)
     hbm = pl.BlockSpec(memory_space=pl.ANY)
     half = lambda *lead: [pltpu.VMEM((*lead, STEP, wide), jnp.bfloat16) for _ in range(n)]
     state = jax.ShapeDtypeStruct(theta.shape, jnp.float32)
     return pl.pallas_call(
         functools.partial(kernel, room, chunks),
         out_shape=(jax.ShapeDtypeStruct(deltas.shape, jnp.bfloat16), state, state, state),
-        in_specs=[hbm, smem, smem, smem, smem, vmem, vmem, vmem],
-        out_specs=(hbm, vmem, vmem, vmem),
+        in_specs=[hbm, smem, smem, smem, smem, hbm, hbm, hbm],
+        out_specs=(hbm, hbm, hbm, hbm),
         scratch_shapes=[
+            [pltpu.VMEM(theta.shape, jnp.float32) for _ in range(3)],
             half(SIDE, SIDE),
             half(SIDE, slots),
             half(SIDE, slots),
@@ -241,11 +261,34 @@
             pltpu.SemaphoreType.DMA(copies),
             pltpu.SemaphoreType.DMA(copies),
             pltpu.SemaphoreType.DMA((2 * n,)),
+            pltpu.SemaphoreType.DMA((n + 1, 3)),
         ],
         compiler_params=pltpu.CompilerParams(
             collective_id=tag, has_side_effects=True, vmem_limit_bytes=48 * 1024 * 1024
         ),
     )(deltas, order, staleness, period, counter, theta, momentum, accum)
+
+
+def settle_kernel(*refs):
+    half = len(refs) // 2
+    for src, dst in zip(refs[:half], refs[half:]):
+        dst[...] = src[...]
+
+
+def settle(*results):
+    def spec(r):
+        shape = (r.shape[0] // SETTLE, *r.shape[1:])
+        return pl.BlockSpec(shape, lambda i: (i,) + (0,) * (r.ndim - 1))
+
+    specs = tuple(spec(r) for r in results)
+    return pl.pallas_call(
+        settle_kernel,
+        grid=(SETTLE,),
+        out_shape=tuple(jax.ShapeDtypeStruct(r.shape, r.dtype) for r in results),
+        in_specs=specs,
+        out_specs=specs,
+        compiler_params=pltpu.CompilerParams(vmem_limit_bytes=48 * 1024 * 1024),
+    )(*results)
 
 
 def local(deltas, order, staleness, period, counter, theta, momentum, accum):
@@ -257,7 +300,8 @@
     args = (blocks, order, staleness, period, counter, theta[0], momentum[0], accum[0])
     branches = [functools.partial(run, room, tag) for tag, room in enumerate(PLANS)]
     fits = (crowd[None, :] <= jnp.array(PLANS)).all(1)
-    fresh, theta, momentum, accum = lax.switch(jnp.argmax(fits).astype(jnp.int32), branches, *args)
+    results = lax.switch(jnp.argmax(fits).astype(jnp.int32), branches, *args)
+    fresh, theta, momentum, accum = settle(*results)
     return (fresh.reshape(deltas.shape), theta[None], momentum[None], accum[None])
 
 

time: 166 us -> 87.9 us (0.53)
  Pallas kernels: 157 us -> 83.8 us
  local copies, waits for them, and re-layouts: 3.99 us -> 0.08 us
    pallas_call x1, Pallas kernels: 157 us -> 80.5 us  [run(): pl.pallas_call(functools.partial(kernel, room, chunks), out_shape=(jax.Sh...]
    unnamed x4 -> x0, local copies, waits for them, and re-layouts: 3.9 us -> none
    pallas_call x0 -> x1, Pallas kernels: none -> 3.22 us  [settle(): pl.pallas_call(settle_kernel, grid=(SETTLE,), out_shape=tuple((jax.ShapeD...]
where the time goes in v4:
time: 87.9 us; the launch traced here: 87.6 us
  Pallas kernels  83.8 us (95%)
  other arithmetic  2.23 us (3%)
  between operations  1.29 us (1%)
    pallas_call x1, Pallas kernels, run(): pl.pallas_call(functools.partial(kernel, room, chunks), out_shape=(jax.Sh...  80.5 us
    pallas_call x1, Pallas kernels, settle(): pl.pallas_call(settle_kernel, grid=(SETTLE,), out_shape=tuple((jax.ShapeD...  3.22 us

profile of v4, /device:TPU:24, one launch (start us, length us, event | category | flops | bytes accessed | tf_op | source)
XLA Modules:
  0.0 87.6 jit_solution(17279389875453562082)
XLA Ops:
  0.6 0.7 fusion
  1.4 0.1 reshape.21
  1.5 0.8 compare_reduce_fusion
  2.3 0.7 iota_reduce_fusion
  3.6 80.8 %conditional.1 = ((bf16[16,64,1536]{2,1,0:T(8,128)(2,1)S(1)}, f32[64,1536]{1,0:T(8,128)S(1)}, f32[64,1536]{1,0:T(8,128)}, f32[64,1536]{1,0:T(8,128)})) conditional(s32[]{:T(128)} %clamp.3, (bf16[16,64,1536]{2,1,0:T(8,128)(2,1)}, s32[4]{0:T(128)}, s32[16]{0:T(128)}, s32[1]{0:T(128)}, s32[1]{0:T(128)}, ...), branch_computations={%region_4.5_spmd, %region_5.6_spmd, %region_6.7_spmd, %region_7.8_... | conditional | bytes 8 | solution.py:303
  3.6 80.5 %branch_0_fun.1 = (bf16[16,64,1536]{2,1,0:T(8,128)(2,1)S(1)}, f32[64,1536]{1,0:T(8,128)S(1)}, f32[64,1536]{1,0:T(8,128)}, f32[64,1536]{1,0:T(8,128)}) custom-call(bf16[16,64,1536]{2,1,0:T(8,128)(2,1)} %get-tuple-element.64.deltas, s32[4]{0:T(128)} %get-tuple-element.65.order, s32[16]{0:T(128)} %get-tuple-element.66.staleness, s32[1]{0:T(128)} %get-tuple-element.67.period, ...), custom_call_target="tpu_custom_call" | custom-call | tf_op jit(solution)/shard_map/cond/branch_0_fun/pallas_call | solution.py:247
  84.4 3.2 %shard_map.120 = (bf16[16,64,1536]{2,1,0:T(8,128)(2,1)}, f32[64,1536]{1,0:T(8,128)}, f32[64,1536]{1,0:T(8,128)}, f32[64,1536]{1,0:T(8,128)}) custom-call(bf16[16,64,1536]{2,1,0:T(8,128)(2,1)S(1)} %get-tuple-element.110.refs_0_, f32[64,1536]{1,0:T(8,128)S(1)} %get-tuple-element.111.refs_1_, f32[64,1536]{1,0:T(8,128)} %get-tuple-element.112.refs_2_, ...), custom_call_target="tpu_custom_call" | custom-call | tf_op jit(solution)/shard_map/pallas_call | solution.py:284
  (2 shorter events, 0.0 us)
